TPU v7x, 256 devices: a whole 4x4x8 slice. The times are simulated.
256 devices in a mesh: ctx: 64 (over z, y, core), head: 4 (over x).
Axes of the slice: x: 4, y: 4, z: 8, core: 2. Of those that a mesh axis runs over, the one named last changes fastest.
Arguments:
- queries: bfloat16 [131072, 2048], P('ctx', 'head'), may hold values from -6 to 6
- keys: bfloat16 [131072, 2048], P('ctx', 'head'), may hold values from -6 to 6
- values: bfloat16 [131072, 2048], P('ctx', 'head'), may hold values from -6 to 6
- out_weight: bfloat16 [2048, 2048], P('head'), may hold values from -0.5 to 0.5
- block_order: int32 [1024], replicated, may hold values from 0 to 1023, as said below
- selection: int32 [1024, 2], P('ctx'), may hold values from 0 to 1023, as said below
Outputs:
- layer_out: bfloat16 [131072, 2048], P('ctx', 'head')
Inputs may be any that keep to these rules, and one draw needn't show every extreme that they name: `block_order`: A permutation of the sequence's blocks; device d of ctx stores blocks d*16 to (d+1)*16 - 1. `selection`: for the stored block s with g = block_order[s], each entry is a sequence block before g, or g itself for an empty entry; the two entries of a row differ unless empty. Over the rows of one device, at most 1 entries that are not empty name blocks stored on any one device. Sequence block 0 is named by a row of every device. The row of sequence block 1023 has an empty second entry.
All inputs are finite; a program needn't handle non-finite values.
Results may differ from a plain program's by a relative error of at most 0.029.
Values may be sent and summed in bfloat16 or wider, within the bound.
A program may use at most 192 MiB of HBM per device.

v0:
```python
import jax
import jax.numpy as jnp
from jax import lax
from jax.sharding import PartitionSpec as P

DH = 128
BLK = 128


NEG_BIG = -1e30


def partial_attention(query_rows, key_rows, value_rows, allowed):
    leading = query_rows.shape[:-2]
    block_rows = query_rows.shape[-2]
    head_count = query_rows.shape[-1] // DH
    q_split = query_rows.reshape(leading + (block_rows, head_count, DH))
    k_split = key_rows.reshape(leading + (block_rows, head_count, DH))
    v_split = value_rows.reshape(leading + (block_rows, head_count, DH))
    scores = jnp.einsum(
        "...qhd,...khd->...hqk", q_split, k_split, preferred_element_type=jnp.float32
    ) * DH ** (-0.5)
    scores = jnp.where(allowed, scores, NEG_BIG)
    row_max = jnp.max(scores, axis=-1, keepdims=True)
    weights = jnp.exp(scores - row_max)
    totals = jnp.sum(weights, axis=-1)
    mixed_out = jnp.einsum(
        "...hqk,...khd->...qhd",
        weights.astype(jnp.bfloat16),
        v_split,
        preferred_element_type=jnp.float32,
    )
    mixed_out = mixed_out / jnp.swapaxes(totals, -1, -2)[..., None]
    log_total = row_max[..., 0] + jnp.log(totals)
    return (mixed_out.reshape(leading + (block_rows, head_count * DH)), log_total)


def spread_heads(weight_map):
    return jnp.repeat(jnp.swapaxes(weight_map, -1, -2), DH, axis=-1)


def combine_parts(own_out, own_log, item_out, item_log, live):
    live_mask = live[:, :, None, None]
    live_log = jnp.where(live_mask, item_log, own_log[:, None])
    row_max = jnp.maximum(own_log, jnp.max(live_log, axis=1))
    own_weight = jnp.exp(own_log - row_max)
    item_weight = jnp.where(live_mask, jnp.exp(live_log - row_max[:, None]), 0.0)
    total = own_weight + jnp.sum(item_weight, axis=1)
    merged = spread_heads(own_weight) * own_out
    merged = merged + jnp.sum(spread_heads(item_weight) * item_out.astype(jnp.float32), axis=1)
    return (merged / spread_heads(total)).astype(jnp.bfloat16)


def shards(queries, keys, values, out_weight, block_order, selection):
    ctx_count = lax.axis_size("ctx")
    my_index = lax.axis_index("ctx")
    local_rows = queries.shape[0]
    width_here = queries.shape[1]
    head_count = width_here // DH
    blocks_here = local_rows // BLK
    item_count = 2 * blocks_here
    capacity = max(1, item_count // ctx_count)
    slot_count = ctx_count * capacity
    total_blocks = block_order.shape[0]
    q_blocks = queries.reshape(blocks_here, BLK, width_here)
    k_blocks = keys.reshape(blocks_here, BLK, width_here)
    v_blocks = values.reshape(blocks_here, BLK, width_here)
    storage_of = (
        jnp.zeros((total_blocks,), jnp.int32)
        .at[block_order]
        .set(jnp.arange(total_blocks, dtype=jnp.int32))
    )
    own_ids = lax.dynamic_slice_in_dim(block_order, my_index * blocks_here, blocks_here)
    wanted = selection.reshape(-1)
    is_live = wanted != jnp.repeat(own_ids, 2)
    wanted_slot = storage_of[wanted]
    target = jnp.where(is_live, wanted_slot // blocks_here, -1)
    local_key = wanted_slot % blocks_here
    order_item = jnp.arange(item_count, dtype=jnp.int32)
    same_target = (target[:, None] == target[None, :]) & (order_item[None, :] < order_item[:, None])
    rank_within = jnp.sum(same_target.astype(jnp.int32), axis=1)
    position = jnp.where(is_live, target * capacity + rank_within, slot_count)
    item_of_slot = jnp.full((slot_count,), -1, jnp.int32).at[position].set(order_item, mode="drop")
    slot_filled = item_of_slot >= 0
    source_item = jnp.maximum(item_of_slot, 0)
    query_send = q_blocks[source_item // 2].reshape(ctx_count, capacity, BLK, width_here)
    key_send = jnp.where(slot_filled, local_key[source_item], 0).reshape(ctx_count, capacity)
    arrived = lax.all_to_all(query_send, "ctx", split_axis=0, concat_axis=0, tiled=True)
    key_index = lax.all_to_all(key_send, "ctx", split_axis=0, concat_axis=0, tiled=True)
    picked_keys = k_blocks[key_index]
    picked_values = v_blocks[key_index]
    out_part, log_part = partial_attention(arrived, picked_keys, picked_values, True)
    remote_out = lax.all_to_all(
        out_part.astype(jnp.bfloat16), "ctx", split_axis=0, concat_axis=0, tiled=True
    )
    remote_log = lax.all_to_all(
        log_part.astype(jnp.bfloat16), "ctx", split_axis=0, concat_axis=0, tiled=True
    ).astype(log_part.dtype)
    flat_out = remote_out.reshape(slot_count, BLK, width_here)
    flat_log = remote_log.reshape(slot_count, head_count, BLK)
    fetch = jnp.minimum(position, slot_count - 1)
    item_out = flat_out[fetch].reshape(blocks_here, 2, BLK, width_here)
    item_log = flat_log[fetch].reshape(blocks_here, 2, head_count, BLK)
    causal = lax.broadcasted_iota(jnp.int32, (BLK, BLK), 0) >= lax.broadcasted_iota(
        jnp.int32, (BLK, BLK), 1
    )
    own_out, own_log = partial_attention(q_blocks, k_blocks, v_blocks, causal)
    attention_layer = combine_parts(
        own_out, own_log, item_out, item_log, is_live.reshape(blocks_here, 2)
    )
    projected = jnp.dot(
        attention_layer.reshape(local_rows, width_here),
        out_weight,
        preferred_element_type=jnp.float32,
    )
    return lax.psum_scatter(projected.astype(jnp.bfloat16), "head", scatter_dimension=1, tiled=True)


def solution(mesh):
    return jax.shard_map(
        shards,
        mesh=mesh,
        in_specs=(
            P("ctx", "head"),
            P("ctx", "head"),
            P("ctx", "head"),
            P("head", None),
            P(),
            P("ctx", None),
        ),
        out_specs=P("ctx", "head"),
        check_vma=False,
    )
```

profile of v0, /device:TPU:1, one launch (start us, length us, event | category | flops | bytes accessed | tf_op | source)
XLA Modules:
  0.0 609.5 jit_solution(17706433240051889287)
XLA Ops:
  6.5 0.8 compare_select_fusion.1
  7.4 0.8 dynamic_slice.3
  8.1 0.8 copy.86
  8.9 0.7 broadcast_compare_fusion
  9.6 0.1 copy.85
  9.7 0.1 ne.109
  9.8 0.1 reshape.333
  9.9 4.3 scatter_custom_fusion
  14.2 0.7 gather_fusion
  14.9 0.2 convert_reduce_fusion
  15.2 0.1 reshape.334
  15.3 0.7 scatter_custom_fusion.1
  16.0 0.8 gather_fusion.2
  16.8 0.7 copy.91
  17.5 13.2 %all-to-all-start.1 = ((s32[64,1,1]{2,1,0:T(1,128)}), s32[64,1,1]{2,1,0:T(1,128)S(1)}, u32[]{:S(2)}, u32[]{:S(2)}) async-start(s32[64,1,1]{2,1,0:T(1,128)} %copy.91), calls=%async_computation.1 | async-start | bytes 65536 | tf_op jit(solution)/shard_map/all_to_all | solution.py:89
  30.7 7.1 %gather_fusion.1 = bf16[64,128,512]{2,1,0:T(8,128)(2,1)} fusion(bf16[16,128,512]{2,1,0:T(8,128)(2,1)} %bitcast.109, s32[1024]{0:T(1024)S(1)} %pad_clamp_fusion.3), kind=kCustom, calls=%fused_computation.1 | custom fusion | bytes 16777472 | tf_op jit(solution)/shard_map/gather | solution.py:86
  37.7 2.2 all-to-all-done.1
  40.0 8.2 %all-to-all-start = ((bf16[64,1,128,512]{3,2,1,0:T(8,128)(2,1)}), bf16[64,1,128,512]{3,2,1,0:T(8,128)(2,1)}, u32[]{:S(2)}, u32[]{:S(2)}) async-start(bf16[64,1,128,512]{3,2,1,0:T(8,128)(2,1)} %bitcast.111), calls=%async_computation | async-start | bytes 16777216 | tf_op jit(solution)/shard_map/all_to_all | solution.py:88
  48.2 1.2 fusion.30
  49.4 7.0 %gather_fusion.3 = bf16[64,128,512]{2,1,0:T(8,128)(2,1)} fusion(bf16[16,128,512]{2,1,0:T(8,128)(2,1)} %bitcast.108, s32[1024]{0:T(1024)S(1)} %pad_clamp_fusion.1), kind=kCustom, calls=%fused_computation.3 | custom fusion | bytes 16777472 | tf_op jit(solution)/shard_map/gather | solution.py:90
  56.5 11.9 %copy.92 = bf16[64,128,512]{1,2,0:T(8,128)(2,1)} copy(bf16[64,128,512]{2,1,0:T(8,128)(2,1)} %gather_fusion.3) | data formatting | bytes 16777216 | tf_op jit(solution)/shard_map/gather | solution.py:90
  68.3 7.0 %gather_fusion.5 = bf16[64,128,512]{2,1,0:T(8,128)(2,1)} fusion(bf16[16,128,512]{2,1,0:T(8,128)(2,1)} %bitcast.110, s32[1024]{0:T(1024)S(1)} %pad_clamp_fusion.1), kind=kCustom, calls=%fused_computation.5 | custom fusion | bytes 16777472 | tf_op jit(solution)/shard_map/gather | solution.py:91
  75.3 11.9 %copy.97 = bf16[64,128,512]{1,2,0:T(8,128)(2,1)} copy(bf16[64,128,512]{2,1,0:T(8,128)(2,1)} %gather_fusion.5) | data formatting | bytes 16777216 | tf_op jit(solution)/shard_map/gather | solution.py:91
  87.2 143.4 %all-to-all-done = bf16[64,1,128,512]{3,2,1,0:T(8,128)(2,1)} async-done(((bf16[64,1,128,512]{3,2,1,0:T(8,128)(2,1)}), bf16[64,1,128,512]{3,2,1,0:T(8,128)(2,1)}, u32[]{:S(2)}, u32[]{:S(2)}) %all-to-all-start) | async-done | bytes 8388640 | tf_op jit(solution)/shard_map/all_to_all | solution.py:88
  230.7 11.9 %copy.90 = bf16[64,1,128,512]{2,3,0,1:T(8,128)(2,1)} copy(bf16[64,1,128,512]{3,2,1,0:T(8,128)(2,1)} %all-to-all-done) | data formatting | bytes 16777216 | tf_op jit(solution)/shard_map/all_to_all | solution.py:88
  242.6 10.9 %multiply_reduce_fusion = (f32[64,4,128]{2,1,0:T(4,128)S(1)}, f32[64,4,128,128]{2,3,1,0:T(8,128)}) fusion(bf16[64,128,4,128]{1,3,2,0:T(8,128)(2,1)} %bitcast.107, bf16[64,128,4,128]{1,3,2,0:T(8,128)(2,1)} %bitcast.106), kind=kOutput, calls=%fused_computation.12 | convolution fusion | flops 1082097664 | bytes 33685504 | tf_op jit(solution)/shard_map/...qhd,...khd->...hqk/dot_general | solution.py:20
  253.5 10.1 %fusion.2 = f32[64,4,128]{2,1,0:T(4,128)S(1)} fusion(f32[64,4,128,128]{2,3,1,0:T(8,128)} %get-tuple-element.16, f32[64,4,128]{2,1,0:T(4,128)S(1)} %get-tuple-element.15), kind=kLoop, calls=%fused_computation.14 | loop fusion | flops 12550144 | bytes 17039360 | tf_op jit(solution)/shard_map/reduce_sum | solution.py:26
  263.6 0.7 fusion.26
  264.2 10.0 %all-to-all-start.2 = ((bf16[64,1,4,128]{3,2,1,0:T(4,128)(2,1)}), bf16[64,1,4,128]{3,2,1,0:T(4,128)(2,1)S(1)}, u32[]{:S(2)}, u32[]{:S(2)}) async-start(bf16[64,1,4,128]{3,2,1,0:T(4,128)(2,1)} %fusion.26), calls=%async_computation.2 | async-start | bytes 131072 | tf_op jit(solution)/shard_map/all_to_all | solution.py:96
  274.2 12.8 %fusion = bf16[64,1,128,4,128]{2,4,3,0,1:T(8,128)(2,1)} fusion(bf16[64,128,4,128]{1,3,2,0:T(8,128)(2,1)} %bitcast.114, f32[64,4,128,128]{2,3,1,0:T(8,128)} %get-tuple-element.16, f32[64,128,4]{1,2,0:T(4,128)S(1)} %bitcast.116, f32[64,4,128]{2,1,0:T(4,128)S(1)} %get-tuple-element.15), kind=kOutput, calls=%fused_computation.10 | convolution fusion | flops 1094713344 | bytes 33816576 | tf_op jit(solution)/shard_map/...hqk,...khd->...qhd/dot_general | solution.py:27
  287.0 10.5 %all-to-all-start.3 = ((bf16[64,1,128,512]{2,3,1,0:T(8,128)(2,1)}), bf16[64,1,128,512]{2,3,1,0:T(8,128)(2,1)}, u32[]{:S(2)}, u32[]{:S(2)}) async-start(bf16[64,1,128,512]{2,3,1,0:T(8,128)(2,1)} %bitcast.113), calls=%async_computation.3 | async-start | bytes 16777216 | tf_op jit(solution)/shard_map/all_to_all | solution.py:93
  297.6 4.0 reshape_reshape.10
  301.5 4.0 reshape_reshape.9
  305.5 4.0 reshape_reshape.11
  309.5 3.8 fusion.11
  313.4 2.0 copy-done.1
  315.3 1.2 fusion.13
  316.6 0.6 gather_fusion.4
  317.2 0.1 select_reduce_fusion
  317.3 0.1 fusion.27
  317.5 162.4 %all-to-all-done.3 = bf16[64,1,128,512]{2,3,1,0:T(8,128)(2,1)} async-done(((bf16[64,1,128,512]{2,3,1,0:T(8,128)(2,1)}), bf16[64,1,128,512]{2,3,1,0:T(8,128)(2,1)}, u32[]{:S(2)}, u32[]{:S(2)}) %all-to-all-start.3) | async-done | bytes 8388640 | tf_op jit(solution)/shard_map/all_to_all | solution.py:93
  479.9 6.4 %gather_fusion.6 = bf16[32,128,512]{1,2,0:T(8,128)(2,1)} fusion(bf16[64,128,512]{1,2,0:T(8,128)(2,1)} %bitcast.29, s32[1024]{0:T(1024)S(1)} %pad_clamp_fusion), kind=kCustom, calls=%fused_computation.6 | custom fusion | bytes 8388736 | tf_op jit(solution)/shard_map/gather | solution.py:102
  486.3 5.9 fusion.4
  492.2 5.3 copy.100
  497.5 8.0 %fusion.10 = bf16[16,128,4,128]{3,1,2,0:T(8,128)(2,1)} fusion(f32[16,128,4,128]{3,1,2,0:T(8,128)} %copy.100, f32[16,4,128,128]{2,3,1,0:T(8,128)} %copy-done.1, bf16[16,128,4,128]{3,2,1,0:T(4,128)(2,1)} %reshape_reshape.11, f32[16,128,4]{1,2,0:T(4,128)S(1)} %get-tuple-element.5, f32[16,128,4]{1,2,0:T(4,128)S(1)} %bitcast.122, ...), kind=kOutput, calls=%fused_computation.26 | convolution fusion | flops 277872640 | bytes 12730368 | tf_op jit(solution)/shard_map/...hqk,...khd->...qhd/dot_general | solution.py:27
  505.6 4.5 copy.101
  510.1 8.5 %convolution_convert_fusion = bf16[2048,2048]{1,0:T(8,128)(2,1)} fusion(bf16[512,2048]{1,0:T(8,128)(2,1)S(1)} %copy-done, bf16[64,8,16,128]{3,2,1,0:T(8,128)(2,1)} %bitcast.115), kind=kOutput, calls=%fused_computation.19 | convolution fusion | flops 4299161600 | bytes 12582912 | tf_op jit(solution)/shard_map/dot_general | solution.py:111
  518.7 84.0 %reduce-scatter.2.cloned.1.call-done = bf16[2048,512]{1,0:T(8,128)(2,1)} async-done(((bf16[2048,2048]{1,0:T(8,128)(2,1)}), bf16[2048,512]{1,0:T(8,128)(2,1)}) %reduce-scatter.2.cloned.1.call-update) | async-done | bytes 2097168 | tf_op jit(solution)/shard_map/reduce_scatter | solution.py:116
  (25 shorter events, 0.3 us)
Async XLA Ops:
  6.5 503.6 %copy-start = (bf16[512,2048]{1,0:T(8,128)(2,1)S(1)}, bf16[512,2048]{1,0:T(8,128)(2,1)}, u32[]{:S(2)}) copy-start(bf16[512,2048]{1,0:T(8,128)(2,1)} %param.9) | copy-start | bytes 6291460
  17.5 22.5 %all-to-all-start.1 = ((s32[64,1,1]{2,1,0:T(1,128)}), s32[64,1,1]{2,1,0:T(1,128)S(1)}, u32[]{:S(2)}, u32[]{:S(2)}) async-start(s32[64,1,1]{2,1,0:T(1,128)} %copy.91), calls=%async_computation.1 | async-start | bytes 65536 | tf_op jit(solution)/shard_map/all_to_all | solution.py:89
  40.0 190.7 %all-to-all-start = ((bf16[64,1,128,512]{3,2,1,0:T(8,128)(2,1)}), bf16[64,1,128,512]{3,2,1,0:T(8,128)(2,1)}, u32[]{:S(2)}, u32[]{:S(2)}) async-start(bf16[64,1,128,512]{3,2,1,0:T(8,128)(2,1)} %bitcast.111), calls=%async_computation | async-start | bytes 16777216 | tf_op jit(solution)/shard_map/all_to_all | solution.py:88
  264.2 22.8 %all-to-all-start.2 = ((bf16[64,1,4,128]{3,2,1,0:T(4,128)(2,1)}), bf16[64,1,4,128]{3,2,1,0:T(4,128)(2,1)S(1)}, u32[]{:S(2)}, u32[]{:S(2)}) async-start(bf16[64,1,4,128]{3,2,1,0:T(4,128)(2,1)} %fusion.26), calls=%async_computation.2 | async-start | bytes 131072 | tf_op jit(solution)/shard_map/all_to_all | solution.py:96
  287.0 192.9 %all-to-all-start.3 = ((bf16[64,1,128,512]{2,3,1,0:T(8,128)(2,1)}), bf16[64,1,128,512]{2,3,1,0:T(8,128)(2,1)}, u32[]{:S(2)}, u32[]{:S(2)}) async-start(bf16[64,1,128,512]{2,3,1,0:T(8,128)(2,1)} %bitcast.113), calls=%async_computation.3 | async-start | bytes 16777216 | tf_op jit(solution)/shard_map/all_to_all | solution.py:93
  297.5 305.1 %reduce-scatter.2.cloned.1.call-start = ((), (), s32[]{:S(2)}) async-start(), calls=%async_computation.5 | async-start | bytes 10485760 | tf_op jit(solution)/shard_map/reduce_scatter | solution.py:116
  313.3 2.0 copy-start.1
Sparse Core Ops, SparseCore 0:
  518.8 83.7 reduce-scatter.1
where the time goes:
time: 611 us; the launch traced here: 609 us
  waiting for transfers between devices  392 us (64%)
  local copies, waits for them, and re-layouts  96.7 us (16%)
  matrix products  44.1 us (7%)
  starting transfers between devices  41.9 us (7%)
  other arithmetic  21.2 us (3%)
  between operations  13.6 us (2%)
    all_to_all x1, waiting for transfers between devices, shards(): lax.all_to_all(out_part.astype(jnp.bfloat16), 'ctx', split_axis=0, concat...  162 us
    all_to_all x1, waiting for transfers between devices, shards(): lax.all_to_all(query_send, 'ctx', split_axis=0, concat_axis=0, tiled=True)  143 us
    reduce_scatter x1, waiting for transfers between devices, shards(): lax.psum_scatter(projected.astype(jnp.bfloat16), 'head', scatter_dimensio...  84 us
    dot_general x2, matrix products, partial_attention(): jnp.einsum('...hqk,...khd->...qhd', weights.astype(jnp.bfloat16), v_split...  20.8 us
    gather x2, local copies, waits for them, and re-layouts, shards(): picked_values = v_blocks[key_index]  18.9 us
    gather x2, local copies, waits for them, and re-layouts, shards(): picked_keys = k_blocks[key_index]  18.9 us
    dot_general x2, matrix products, partial_attention(): jnp.einsum('...qhd,...khd->...hqk', q_split, k_split, preferred_element_t...  14.7 us
    all_to_all x1, starting transfers between devices, shards(): lax.all_to_all(key_send, 'ctx', split_axis=0, concat_axis=0, tiled=True)  13.2 us
  transfers between devices with their start and end apart: 5, of which 4 were waited for; matrix products, arithmetic and copies ran while one was open for 13% of the time, Pallas kernels for 0%

commit v1 on v0

v1 whole, which is shorter than its diff:
```python
import functools

import jax
import jax.numpy as jnp
from jax import lax
from jax.experimental import pallas as pl
from jax.experimental.pallas import tpu as pltpu
from jax.sharding import PartitionSpec as P

MESH = pl.DeviceIdType.MESH
DH = 128
BLK = 128
HEADS = 4
BLOCKS = 16
ROWS = BLOCKS * BLK
PLANES = 8
MATES = 8
NZ = PLANES - 1
SCALE = DH ** (-0.5)
FAST = (6, 3, 3)
FULL = (8, 0, 0)

T_SEND, T_KEY, T_EXC, T_IN_Q, T_IN_K = 0, 56, 112, 120, 128
T_OUT, T_LOG, T_LIVE, T_BACK, T_BACK_LOG = 136, 168, 200, 232, 240
LOG_BACK, LOG_IN = 56, 112


def bf(x):
    return x.astype(jnp.bfloat16)


def attend(query, key, value_t, allowed=None):
    scores = lax.dot_general(
        key, query, (((1,), (1,)), ((), ())), preferred_element_type=jnp.float32
    ) * SCALE
    if allowed is not None:
        scores = jnp.where(allowed, scores, -1e30)
    top = jnp.max(scores, axis=0, keepdims=True)
    weights = jnp.exp(scores - top)
    total = jnp.sum(weights, axis=0, keepdims=True)
    out = jnp.dot(value_t, bf(weights), preferred_element_type=jnp.float32)
    return out / total, top + jnp.log(total)


def split_logs(logs, count):
    rows = list(logs) + [jnp.zeros_like(logs[0])] * (8 - count)
    whole = jnp.concatenate(rows, axis=0)
    high = bf(whole)
    low = bf(whole - high.astype(jnp.float32))
    return jnp.concatenate([high, low], axis=0)


def join_logs(tile):
    tile = tile.astype(jnp.float32)
    return tile[0:8] + tile[8:16]


def layer_kernel(
    cap, spare, back,
    table, q_hbm, k_hbm, v_hbm, w_hbm, o_ref, kv_far,
    q_own, q_all, kv_own, v_raw, q_out, q_in, o_in, o_all, exc_out, exc_in, back_out, back_in, in_plane, kv_buf,
    own_out, own_log, logs, att, wg, acc,
    load_sem, w_sem, qs_sem, qr_sem, os_sem, or_sem, es_sem, er_sem, bs_sem, br_sem, ks_sem, kr_sem, kl_sem,
    xs_sem, xr_sem,
):
    me = lax.axis_index("ctx")
    x = lax.axis_index("head")
    z = me // MATES
    y = (me % MATES) // 2
    core = me % 2
    msg = cap * BLK
    base_back = NZ * cap
    base_in = NZ * (cap + back)

    def at(dz, dy, dk, dx):
        ctx = ((z + dz) % PLANES) * MATES + ((y + dy) % 4) * 2 + (core + dk) % 2
        return (ctx, (x + dx) % HEADS)

    mates = [(dy, dk) for dy in range(4) for dk in range(2)][1:]

    def remote(src, dst, send, recv, device):
        return pltpu.make_async_remote_copy(
            src_ref=src, dst_ref=dst, send_sem=send, recv_sem=recv, device_id=device, device_id_type=MESH
        )

    def loads(h):
        cols = pl.ds(h * DH, DH)
        return [
            pltpu.make_async_copy(k_hbm.at[:, :, cols], kv_own.at[h, 0], load_sem.at[h, 0]),
            pltpu.make_async_copy(v_hbm.at[:, :, cols], v_raw.at[h], load_sem.at[h, 1]),
            pltpu.make_async_copy(q_hbm.at[:, :, cols], q_own.at[h], load_sem.at[h, 2]),
        ]

    for h in range(HEADS):
        for copy in loads(h):
            copy.start()
    own_w = pltpu.make_async_copy(
        w_hbm.at[:, pl.ds(pl.multiple_of(x * 512, 512), 512)], wg.at[0], w_sem.at[0, 0]
    )
    own_w.start()

    barrier = pltpu.get_barrier_semaphore()
    greet = [at(d, 0, 0, 0) for d in range(1, PLANES)]
    greet += [at(0, dy, dk, 0) for dy, dk in mates] + [at(0, 0, 0, d) for d in range(1, HEADS)]
    for device in greet:
        pl.semaphore_signal(barrier, inc=1, device_id=device, device_id_type=MESH)
    pl.semaphore_wait(barrier, len(greet))

    def w_copy(d):
        cols = pl.ds(pl.multiple_of(((x + d) % HEADS) * 512, 512), 512)
        return remote(w_hbm.at[:, cols], wg.at[HEADS - d], w_sem.at[0, d], w_sem.at[1, HEADS - d], at(0, 0, 0, d))

    def kv_near(h, dy):
        return remote(kv_own.at[h], kv_far.at[h, 2 * ((4 - dy) % 4)], ks_sem.at[h, dy], kr_sem.at[h, 2 * ((4 - dy) % 4)],
                      at(0, dy, 0, 0))

    def kv_next(h, part):
        dy, slot = (1, 6) if part == 0 else (3, 2)
        return remote(kv_far.at[h, slot, part], kv_far.at[h, 4, part], ks_sem.at[h, 4 + part],
                      kr_sem.at[h, 8 + part], at(0, dy, 0, 0))

    def kv_mate(h, dy):
        src = kv_own.at[h] if dy == 0 else kv_far.at[h, 2 * dy]
        return remote(src, kv_far.at[h, 2 * dy + 1], ks_sem.at[h, 6 + dy], kr_sem.at[h, 2 * dy + 1], at(0, 0, 1, 0))

    def exc_copy(h, n):
        dy, dk = mates[n]
        rel = ((4 - dy) % 4) * 2 + dk - 1
        return remote(exc_out.at[h], exc_in.at[h, rel], es_sem.at[h, n], er_sem.at[h, rel], at(0, dy, dk, 0))

    def q_copy(h, n):
        return remote(q_out.at[h, n], q_in.at[h, n, pl.ds(0, msg)], qs_sem.at[h, n], qr_sem.at[h, n], at(n + 1, 0, 0, 0))

    def o_copy(h, n):
        return remote(q_in.at[h, n], o_in.at[h, n], os_sem.at[h, n], or_sem.at[h, n], at(PLANES - 1 - n, 0, 0, 0))

    def back_copy(h, n):
        dy, dk = mates[n]
        rel = ((4 - dy) % 4) * 2 + dk - 1
        return remote(back_out.at[h], back_in.at[h, rel], bs_sem.at[h, n], br_sem.at[h, rel], at(0, dy, dk, 0))

    def x_copy(h, d):
        return remote(att.at[0, h], att.at[HEADS - d, h], xs_sem.at[h, d], xr_sem.at[h, HEADS - d], at(0, 0, 0, d))

    for h in range(HEADS):
        for copy in loads(h):
            copy.wait()

    @pl.loop(0, HEADS)
    def _(h):
        @pl.loop(0, BLOCKS)
        def _(b):
            kv_own[h, 1, b] = v_raw[h, b].T

        if spare:
            for e in range(spare):
                exc_out[h, e] = q_own[h, table[T_EXC + e]]
            for n in range(len(mates)):
                exc_copy(h, n).start()
        kv_near(h, 1).start()
        kv_near(h, 3).start()
        kv_mate(h, 0).start()

    for d in range(1, HEADS):
        w_copy(d).start()

    @pl.loop(0, HEADS)
    def _(h):
        if spare:
            for n in range(len(mates)):
                exc_copy(h, n).wait_recv()
            for n in range(len(mates)):
                for e in range(spare):
                    q_all[BLOCKS + n * spare + e] = exc_in[h, n, e]

        @pl.loop(0, BLOCKS)
        def _(b):
            q_all[b] = q_own[h, b]

        @pl.loop(0, NZ)
        def _(n):
            for i in range(cap):
                q_out[h, n, pl.ds(i * BLK, BLK), :] = q_all[table[T_SEND + n * 8 + i]]
            q_copy(h, n).start()

    def kv_first(h):
        for part, slot, dy in ((0, 6, 1), (1, 2, 3)):
            kv_near(h, dy).wait_recv()
            kv_next(h, part).start()
            kv_mate(h, 4 - dy).start()

    def kv_last(h):
        kv_next(h, 0).wait_recv()
        kv_next(h, 1).wait_recv()
        kv_mate(h, 2).start()
        own = pltpu.make_async_copy(kv_own.at[h], kv_buf.at[:, pl.ds(0, BLOCKS)], kl_sem.at[0])
        own.start()
        copies = [
            pltpu.make_async_copy(kv_far.at[h, n], kv_buf.at[:, pl.ds(n * BLOCKS, BLOCKS)], kl_sem.at[n])
            for n in range(1, MATES)
        ]
        for dy in (1, 2, 3):
            copies[2 * dy - 1].start()
        for dy in range(4):
            kv_mate(h, dy).wait_recv()
            copies[2 * dy].start()
        own.wait()
        for copy in copies:
            copy.wait()

    def kv_block(number):
        return kv_buf[0, number], kv_buf[1, number]

    def far_blocks(h):
        @pl.loop(0, NZ)
        def _(n):
            q_copy(h, n).wait_recv()
            outs, tops = [], []
            for i in range(cap):
                query = q_in[h, n, pl.ds(i * BLK, BLK), :]
                out, top = attend(query, *kv_block(table[T_KEY + n * 8 + i]))
                outs.append(bf(out))
                tops.append(top)
            for i in range(cap):
                q_in[h, n, pl.ds(i * BLK, BLK), :] = outs[i]
            q_in[h, n, pl.ds(msg, 16), :] = split_logs(tops, cap)
            o_copy(h, n).start()

        for j in range(MATES):
            out, top = attend(q_own[h, table[T_IN_Q + j]], *kv_block(table[T_IN_K + j]))
            in_plane[h % 2, j] = bf(out)
            logs[h, LOG_IN + j] = top

    def merge(h):
        causal = lax.broadcasted_iota(jnp.int32, (BLK, BLK), 0) <= lax.broadcasted_iota(jnp.int32, (BLK, BLK), 1)

        @pl.loop(0, BLOCKS // 2)
        def _(pair):
            for half in range(2):
                b = pair * 2 + half
                out, top = attend(q_own[h, b], kv_own[h, 0, b], kv_own[h, 1, b], causal)
                own_out[b] = out
                own_log[b] = top

        @pl.loop(0, MATES)
        def _(j):
            o_all[base_in + j] = in_plane[h % 2, j]

        @pl.loop(0, NZ)
        def _(n):
            o_copy(h, n).wait_recv()
            both = join_logs(o_in[h, n, pl.ds(msg, 16), :])
            for i in range(cap):
                o_all[n * cap + i] = o_in[h, n, pl.ds(i * BLK, BLK), :]
                logs[h, n * 8 + i] = both[i : i + 1]

        if back:
            tops = []
            for f in range(back):
                back_out[h, pl.ds(f * BLK, BLK), :] = o_all[table[T_BACK + f]]
                tops.append(logs[h, table[T_BACK_LOG + f]])
            back_out[h, pl.ds(back * BLK, 16), :] = split_logs(tops, back)
            for n in range(len(mates)):
                back_copy(h, n).start()
            for n in range(len(mates)):
                back_copy(h, n).wait_recv()
            for n in range(len(mates)):
                both = join_logs(back_in[h, n, pl.ds(back * BLK, 16), :])
                for f in range(back):
                    o_all[base_back + n * back + f] = back_in[h, n, pl.ds(f * BLK, BLK), :]
                    logs[h, LOG_BACK + n * 8 + f] = both[f : f + 1]

        @pl.loop(0, BLOCKS)
        def _(b):
            rows = pl.ds(pl.multiple_of(b * BLK, BLK), BLK)
            first = own_log[b]
            others, parts = [], []
            for j in range(2):
                item = b * 2 + j
                dead = (table[T_LIVE + item] - 1).astype(jnp.float32) * 1e30
                others.append(logs[h, table[T_LOG + item]] + dead)
                parts.append(o_all[table[T_OUT + item]].astype(jnp.float32))
            top = jnp.maximum(first, jnp.maximum(others[0], others[1]))
            weight = jnp.exp(first - top)
            total, merged = weight, weight * own_out[b]
            for other, part in zip(others, parts):
                weight = jnp.exp(other - top)
                total = total + weight
                merged = merged + weight * part
            att[0, h, rows, :] = bf(merged / total).T

        for d in range(1, HEADS):
            x_copy(h, d).start()

    def project(h):
        for d in range(1, HEADS):
            x_copy(h, d).wait_recv()
        weights = jnp.concatenate([wg[g, pl.ds(pl.multiple_of(h * DH, DH), DH), :] for g in range(HEADS)], axis=0)

        @pl.loop(0, ROWS // 256)
        def _(r):
            rows = pl.ds(pl.multiple_of(r * 256, 256), 256)
            left = jnp.concatenate([att[g, h, rows, :] for g in range(HEADS)], axis=1)
            acc[rows, :] = acc[rows, :] + jnp.dot(left, weights, preferred_element_type=jnp.float32)

    acc[...] = jnp.zeros_like(acc)
    own_w.wait()
    for d in range(1, HEADS):
        w_copy(d).wait_recv()
    kv_first(0)

    @pl.loop(0, HEADS + 2)
    def _(step):
        @pl.when(step + 1 < HEADS)
        def _():
            kv_first(step + 1)

        @pl.when(step < HEADS)
        def _():
            kv_last(step)
            far_blocks(step)

        @pl.when(jnp.logical_and(step >= 1, step <= HEADS))
        def _():
            merge(step - 1)

        @pl.when(step >= 2)
        def _():
            project(step - 2)

    @pl.loop(0, ROWS // 256)
    def _(r):
        rows = pl.ds(pl.multiple_of(r * 256, 256), 256)
        o_ref[rows, :] = bf(acc[rows, :])

    for d in range(1, HEADS):
        w_copy(d).wait_send()

    @pl.loop(0, HEADS)
    def _(h):
        kv_near(h, 1).wait_send()
        kv_near(h, 3).wait_send()
        for part in range(2):
            kv_next(h, part).wait_send()
        for dy in range(4):
            kv_mate(h, dy).wait_send()
        for n in range(NZ):
            q_copy(h, n).wait_send()
            o_copy(h, n).wait_send()
        for n in range(len(mates)):
            if spare:
                exc_copy(h, n).wait_send()
            if back:
                back_copy(h, n).wait_send()
        for d in range(1, HEADS):
            x_copy(h, d).wait_send()


def layer(sizes, number, table, queries, keys, values, out_weight):
    cap, spare, back = sizes
    msg = cap * BLK
    tile = (BLK, DH)
    b16 = jnp.bfloat16
    dma = pltpu.SemaphoreType.DMA
    any_space = pl.BlockSpec(memory_space=pl.ANY)
    out, _ = pl.pallas_call(
        functools.partial(layer_kernel, cap, spare, back),
        name=f"layer_{cap}",
        out_shape=(
            jax.ShapeDtypeStruct((ROWS, 512), b16),
            jax.ShapeDtypeStruct((HEADS, MATES, 2, BLOCKS) + tile, b16),
        ),
        in_specs=[pl.BlockSpec(memory_space=pltpu.SMEM)] + [any_space] * 4,
        out_specs=(pl.BlockSpec(memory_space=pltpu.VMEM), any_space),
        scratch_shapes=[
            pltpu.VMEM((HEADS, BLOCKS) + tile, b16),
            pltpu.VMEM((BLOCKS + NZ * spare,) + tile, b16),
            pltpu.VMEM((HEADS, 2, BLOCKS) + tile, b16),
            pltpu.VMEM((HEADS, BLOCKS) + tile, b16),
            pltpu.VMEM((HEADS, NZ, msg, DH), b16),
            pltpu.VMEM((HEADS, NZ, msg + 16, DH), b16),
            pltpu.VMEM((HEADS, NZ, msg + 16, DH), b16),
            pltpu.VMEM((NZ * (cap + back) + MATES,) + tile, b16),
            pltpu.VMEM((HEADS, max(spare, 1)) + tile, b16),
            pltpu.VMEM((HEADS, NZ, max(spare, 1)) + tile, b16),
            pltpu.VMEM((HEADS, back * BLK + 16, DH), b16),
            pltpu.VMEM((HEADS, NZ, back * BLK + 16, DH), b16),
            pltpu.VMEM((2, MATES) + tile, b16),
            pltpu.VMEM((2, MATES * BLOCKS) + tile, b16),
            pltpu.VMEM((BLOCKS,) + tile, jnp.float32),
            pltpu.VMEM((BLOCKS, 1, DH), jnp.float32),
            pltpu.VMEM((HEADS, 120, 1, DH), jnp.float32),
            pltpu.VMEM((HEADS, HEADS, ROWS, DH), b16),
            pltpu.VMEM((HEADS, 512, 512), b16),
            pltpu.VMEM((ROWS, 512), jnp.float32),
            dma((HEADS, 3)), dma((2, HEADS)),
            dma((HEADS, NZ)), dma((HEADS, NZ)), dma((HEADS, NZ)), dma((HEADS, NZ)),
            dma((HEADS, NZ)), dma((HEADS, NZ)), dma((HEADS, NZ)), dma((HEADS, NZ)),
            dma((HEADS, 10)), dma((HEADS, 10)), dma((MATES,)),
            dma((HEADS, HEADS)), dma((HEADS, HEADS)),
        ],
        compiler_params=pltpu.CompilerParams(
            collective_id=number, has_side_effects=True, vmem_limit_bytes=63 << 20
        ),
    )(table, *[array.reshape(BLOCKS, BLK, -1) for array in (queries, keys, values)], out_weight)
    return out


def total(mask, value, axes):
    return jnp.sum(jnp.where(mask, value, 0), axis=axes)


def route(places, cap, spare, back):
    eight = jnp.arange(8, dtype=jnp.int32)
    item = jnp.arange(32, dtype=jnp.int32)
    plane = jnp.where(places >= 0, places // 128, -1)
    source = eight[:, None, None]
    goes = plane[..., None] == eight
    away = (plane >= 0) & (plane != source)
    count = jnp.sum(goes, axis=2, dtype=jnp.int32)
    earlier = item[None, :] < item[:, None]
    rank = jnp.sum((plane[..., None, :] == plane[..., :, None]) & earlier, axis=-1, dtype=jnp.int32)
    over = away & (rank >= cap)
    spare_rank = jnp.sum(over[..., None, :] & earlier, axis=-1, dtype=jnp.int32)
    apart = eight[:, None, None] != eight
    over_count = jnp.where(apart, jnp.maximum(count - cap, 0), 0)
    room = jnp.where(apart, jnp.maximum(cap - count, 0), 0)
    before = eight[None, :] < eight[:, None]
    over_before = total(before[None, :, :, None], over_count[:, None], 2)
    order = (eight[:, None] - eight[None, :]) % 8
    first = order[None, :, :] < order[:, None, :]
    room_before = total(first[None], room[:, None], 2)
    turn = total(goes, over_before[:, :, None, :], -1) + rank - cap
    mine = goes[:, :, :, None, :]
    low = total(mine, room_before[:, None, None], -1)
    size = total(mine, room[:, None, None], -1)
    filled = total(mine, count[:, None, None], -1)
    turn8 = turn[..., None]
    hit = over[..., None] & (low <= turn8) & (turn8 < low + size)
    carrier = jnp.where(over, total(hit, eight, -1), eight[None, :, None])
    slot = jnp.where(over, total(hit, filled + turn8 - low, -1), rank)
    flat_over, flat_carrier = over.reshape(8, 256), jnp.where(over, carrier, -1).reshape(8, 256)
    flat = jnp.arange(256, dtype=jnp.int32)
    same = flat_over[:, None, :] & (flat_carrier[:, None, :] == flat_carrier[:, :, None])
    back_rank = jnp.sum(same & (flat[None, :] < flat[:, None]), axis=-1, dtype=jnp.int32).reshape(8, 8, 32)
    fits = ~over | (jnp.any(hit, axis=-1) & (spare_rank < spare) & (back_rank < back))
    return plane, rank, over, spare_rank, carrier, slot, back_rank, jnp.all(fits)


def make_table(places, routed, me, cap, spare, back):
    plane, rank, over, spare_rank, carrier, slot, back_rank, _ = routed
    eight = jnp.arange(8, dtype=jnp.int32)
    item = jnp.arange(32, dtype=jnp.int32)
    z, w = me // 8, me % 8

    def relative(device):
        return ((device // 2 - w // 2) % 4) * 2 + (device - w) % 2

    def here(array):
        return lax.dynamic_index_in_dim(array, z, 0, keepdims=False)

    def own(array):
        return lax.dynamic_index_in_dim(here(array), w, 0, keepdims=False)

    shift = jnp.arange(7, dtype=jnp.int32)[:, None, None, None]
    step = (plane - z) % 8 - 1
    key = relative((places % 128) // 16) * 16 + places % 16

    plane_h, over_h, spare_h, carrier_h, slot_h, back_h, step_h = map(
        here, (plane, over, spare_rank, carrier, slot, back_rank, step)
    )
    sent = (plane_h >= 0) & (plane_h != z) & (carrier_h == w)
    source = jnp.where(
        eight[:, None] == w, item[None, :] // 2, 16 + (relative(eight)[:, None] - 1) * spare + spare_h
    )
    slots = eight[None, :, None, None]
    send = total(sent & (step_h == shift) & (slot_h == slots), source, (-1, -2))
    comes = (plane == z) & (eight[:, None, None] != z) & (carrier == w)
    from_step = ((z - eight) % 8 - 1)[:, None, None]
    arrive = total(comes & (from_step == shift[..., None]) & (slot == slots[..., None]), key, (-1, -2, -3))

    plane_o, over_o, spare_o, carrier_o, slot_o, back_o, step_o, rank_o, key_o = map(
        own, (plane, over, spare_rank, carrier, slot, back_rank, step, rank, key)
    )
    exc = total(over_o & (spare_o == eight[:, None]), item // 2, -1)
    inside = plane_o == z
    local = inside & (rank_o == eight[:, None])
    in_q = total(local, item // 2, -1)
    in_k = total(local, key_o, -1)
    rel = relative(carrier_o) - 1
    place = jnp.where(over_o, 7 * cap + rel * back + back_o, step_o * cap + slot_o)
    place = jnp.where(inside, 7 * (cap + back) + rank_o, place)
    log = jnp.where(over_o, LOG_BACK + rel * 8 + back_o, step_o * 8 + slot_o)
    log = jnp.where(inside, LOG_IN + rank_o, log)
    live = plane_o >= 0
    place, log = jnp.where(live, place, 0), jnp.where(live, log, 0)
    foreign = over_h & (carrier_h == w) & (back_h == eight[:, None, None])
    back_place = total(foreign, step_h * cap + slot_h, (-1, -2))
    back_log = total(foreign, step_h * 8 + slot_h, (-1, -2))
    pieces = [send.reshape(-1), arrive.reshape(-1), exc, in_q, in_k, place, log, live, back_place, back_log]
    return jnp.concatenate([piece.astype(jnp.int32) for piece in pieces])


def shards(queries, keys, values, out_weight, block_order, selection):
    me = lax.axis_index("ctx")
    stored = jnp.arange(block_order.shape[0], dtype=jnp.int32)
    wanted = selection.reshape(-1)
    own_ids = lax.dynamic_slice_in_dim(block_order, me * BLOCKS, BLOCKS)
    where_stored = total(wanted[:, None] == block_order[None, :], stored[None, :], -1)
    mine = jnp.where(wanted != jnp.repeat(own_ids, 2), where_stored, -1)
    places = lax.all_gather(mine, "ctx").reshape(8, 8, 32)
    arrays = (queries, keys, values, out_weight)
    routed = route(places, *FAST)

    def fast():
        return layer(FAST, 0, make_table(places, routed, me, *FAST), *arrays)

    def full():
        return layer(FULL, 1, make_table(places, route(places, *FULL), me, *FULL), *arrays)

    return lax.cond(routed[-1], fast, full)


def solution(mesh):
    return jax.shard_map(
        shards,
        mesh=mesh,
        in_specs=(
            P("ctx", "head"),
            P("ctx", "head"),
            P("ctx", "head"),
            P("head", None),
            P(),
            P("ctx", None),
        ),
        out_specs=P("ctx", "head"),
        check_vma=False,
    )
```

time: 611 us -> 413 us (0.68)
  waiting for transfers between devices: 392 us -> 0 us
  Pallas kernels: 0 us -> 340 us
  local copies, waits for them, and re-layouts: 96.7 us -> 9.74 us
  blocking collectives: 0 us -> 44.2 us
  matrix products: 44.1 us -> 0 us
  starting transfers between devices: 41.9 us -> 0 us
  between operations: 13.6 us -> 0.86 us
    pallas_call x0 -> x1, Pallas kernels: none -> 340 us  [layer(): pl.pallas_call(functools.partial(layer_kernel, cap, spare, back), name=f'...]
    all_to_all x4 -> x0, waiting for transfers between devices: 308 us -> none  [the longest x1 162 us: shards(): lax.all_to_all(out_part.astype(jnp.bfloat16), 'ctx', split_axis=0, concat...]
    reduce_scatter x1 -> x0, waiting for transfers between devices: 84 us -> none  [shards(): lax.psum_scatter(projected.astype(jnp.bfloat16), 'head', scatter_dimensio...]
    gather x9 -> x0, local copies, waits for them, and re-layouts: 53.3 us -> none  [the longest x2 18.9 us: shards(): picked_values = v_blocks[key_index]]
    all_gather x0 -> x1, blocking collectives: none -> 44.2 us  [shards(): places = lax.all_gather(mine, 'ctx').reshape(8, 8, 32)]
    dot_general x5 -> x0, matrix products: 44.1 us -> none  [the longest x2 20.8 us: partial_attention(): jnp.einsum('...hqk,...khd->...qhd', weights.astype(jnp.bfloat16), v_split...]
    all_to_all x4 -> x0, starting transfers between devices: 41.8 us -> none  [the longest x1 13.2 us: shards(): lax.all_to_all(key_send, 'ctx', split_axis=0, concat_axis=0, tiled=True)]
    all_to_all x2 -> x0, local copies, waits for them, and re-layouts: 12.6 us -> none  [the longest x1 11.9 us: shards(): lax.all_to_all(query_send, 'ctx', split_axis=0, concat_axis=0, tiled=True)]
  transfers between devices with their start and end apart: 5 -> 0, of which waited for: 4 -> 0; matrix products, arithmetic and copies ran while one was open for 13% -> 0% of each run, Pallas kernels for 0% -> 0%
where the time goes in v1:
time: 413 us; the launch traced here: 412 us
  Pallas kernels  340 us (82%)
  blocking collectives  44.2 us (11%)
  other arithmetic  17.4 us (4%)
  local copies, waits for them, and re-layouts  9.74 us (2%)
    pallas_call x1, Pallas kernels, layer(): pl.pallas_call(functools.partial(layer_kernel, cap, spare, back), name=f'...  340 us
    all_gather x1, blocking collectives, shards(): places = lax.all_gather(mine, 'ctx').reshape(8, 8, 32)  44.2 us
    reduce_sum x11, other arithmetic, total(): return jnp.sum(jnp.where(mask, value, 0), axis=axes)  8.92 us

profile of v1, /device:TPU:1, one launch (start us, length us, event | category | flops | bytes accessed | tf_op | source)
XLA Modules:
  0.0 412.2 jit_solution(10550561578010611743)
XLA Ops:
  0.0 0.8 dynamic_slice.128
  0.8 0.7 broadcast_compare_fusion.6
  1.5 0.1 copy.15
  1.6 0.1 ne.657
  1.7 0.1 broadcast_in_dim.484
  1.8 0.1 ne.662
  1.9 0.8 copy.16
  2.6 0.1 eq.488
  2.7 0.9 select_reduce_fusion.29
  3.6 44.2 %all-gather = s32[64,1,32]{2,1,0:T(1,128)S(1)} all-gather(s32[1,1,32]{2,1,0:T(1,128)S(1)} %fusion.109), channel_id=1, replica_groups=mesh['ctx'=64,'head'=4] {'ctx'}, dimensions={0}, use_global_device_ids=true | all-gather | bytes 8320 | tf_op jit(solution)/shard_map/all_gather | solution.py:511
  47.9 0.5 broadcast.1426
  48.4 0.7 reduce.4
  49.1 0.1 reshape.993
  49.2 1.4 convert_reduce_fusion.6
  50.7 0.0 copy-start
  50.7 0.1 ge.136
  50.8 1.2 convert_reduce_fusion.5
  52.0 1.2 convert_reduce_fusion.7
  53.1 0.6 broadcast_in_dim.486
  53.8 0.2 select_reduce_fusion.27
  54.0 0.2 select_reduce_fusion.26
  54.1 0.0 copy-done
  54.1 0.0 copy-done.2
  54.3 1.5 select_reduce_fusion.23
  55.8 0.2 fusion.116
  55.9 0.1 select_reduce_fusion.25
  56.0 0.1 reduce_sum.372
  56.1 0.8 convert_reduce_fusion.4
  57.0 0.0 copy-start.7
  57.0 0.1 lt.339
  57.1 0.7 fusion.98
  58.5 1.6 broadcast_in_dim.476
  60.1 349.1 %conditional.1 = (bf16[2048,512]{1,0:T(8,128)(2,1)}) conditional(s32[]{:T(128)} %convert_element_type.38, (s32[8,8,32]{2,1,0:T(8,128)S(1)}, s32[]{:T(128)}, bf16[2048,512]{1,0:T(8,128)(2,1)}, bf16[2048,512]{1,0:T(8,128)(2,1)}, bf16[2048,512]{1,0:T(8,128)(2,1)}, /*index=5*/bf16[512,2048]{1,0:T(8,128)(2,1)}) %tuple.60, (s32[]{:T(128)}, ...), branch_computations={%region_13.32_spmd, %region_32.42_spmd} | conditional | flops 4858537 | bytes 1207596 | solution.py:521
  60.1 0.9 compare_and_fusion.1
  61.1 0.1 fusion.45
  61.2 0.8 reshape.986
  62.0 0.1 broadcast_and_fusion.1
  62.2 2.5 select_reduce_fusion.14
  64.7 0.2 select_reduce_fusion.16
  64.9 0.9 select_reduce_fusion.20
  65.9 0.4 select_reduce_fusion.18
  66.3 1.1 select_reduce_fusion.17
  67.4 0.1 reshape.984
  67.5 1.1 select_reduce_fusion.15
  68.6 0.1 reshape.985
  68.7 0.7 concatenate.5.table
  69.4 339.8 %layer_6.2 = (bf16[2048,512]{1,0:T(8,128)(2,1)}, bf16[4,8,2,16,128,128]{5,4,3,2,1,0:T(8,128)(2,1)}) custom-call(s32[248]{0:T(256)} %concatenate.5.table, bf16[16,128,512]{2,1,0:T(8,128)(2,1)} %bitcast.34.q_hbm, bf16[16,128,512]{2,1,0:T(8,128)(2,1)} %bitcast.35.k_hbm, bf16[16,128,512]{2,1,0:T(8,128)(2,1)} %bitcast.36.v_hbm, ...), custom_call_target="tpu_custom_call" | custom-call | tf_op jit(solution)/shard_map/cond/branch_1_fun/layer_6/pallas_call | solution.py:366
  409.2 3.0 copy.20
  (49 shorter events, 0.6 us)
Async XLA Ops:
  50.7 3.5 copy-start
  53.1 1.0 copy-start.2
  56.0 1.8 copy-start.3
  57.0 0.8 copy-start.7
  60.1 1.9 copy-start.4
  60.1 1.9 copy-start.6
  60.1 4.7 %copy-start.1 = (s32[8,8,32]{2,1,0:T(8,128)S(1)}, s32[8,8,32]{2,1,0:T(8,128)}, u32[]{:S(2)}) copy-start(s32[8,8,32]{2,1,0:T(8,128)} %get-tuple-element.142) | copy-start | bytes 24580 | tf_op jit(solution)/shard_map/cond
  62.0 2.8 copy-start.5

commit v2 on v1

--- a/solution.py
+++ b/solution.py
@@ -17,8 +17,7 @@
 MATES = 8
 NZ = PLANES - 1
 SCALE = DH ** (-0.5)
-FAST = (6, 3, 3)
-FULL = (8, 0, 0)
+SIZES = ((5, 0, 4, 5), (5, 1, 4, 5), (8, 0, 0, 0))
 
 T_SEND, T_KEY, T_EXC, T_IN_Q, T_IN_K = 0, 56, 112, 120, 128
 T_OUT, T_LOG, T_LIVE, T_BACK, T_BACK_LOG = 136, 168, 200, 232, 240
@@ -56,11 +55,11 @@
 
 
 def layer_kernel(
-    cap, spare, back,
+    cap, extra, spare, back,
     table, q_hbm, k_hbm, v_hbm, w_hbm, o_ref, kv_far,
-    q_own, q_all, kv_own, v_raw, q_out, q_in, o_in, o_all, exc_out, exc_in, back_out, back_in, in_plane, kv_buf,
+    q_own, q_all, kv_own, q_out, q_in, o_in, qx_out, qx_in, ox_in, o_all, exc_out, exc_in, back_out, back_in, in_plane, kv_buf,
     own_out, own_log, logs, att, wg, acc,
-    load_sem, w_sem, qs_sem, qr_sem, os_sem, or_sem, es_sem, er_sem, bs_sem, br_sem, ks_sem, kr_sem, kl_sem,
+    load_sem, w_sem, qs_sem, qr_sem, os_sem, or_sem, qxs_sem, qxr_sem, oxs_sem, oxr_sem, es_sem, er_sem, bs_sem, br_sem, ks_sem, kr_sem, kl_sem,
     xs_sem, xr_sem,
 ):
     me = lax.axis_index("ctx")
@@ -69,8 +68,12 @@
     y = (me % MATES) // 2
     core = me % 2
     msg = cap * BLK
-    base_back = NZ * cap
-    base_in = NZ * (cap + back)
+    base_extra = NZ * cap
+    base_back = base_extra + 4 * extra
+    base_in = base_back + NZ * back
+
+    def more(n):
+        return (n + core) % 2 == 0
 
     def at(dz, dy, dk, dx):
         ctx = ((z + dz) % PLANES) * MATES + ((y + dy) % 4) * 2 + (core + dk) % 2
@@ -83,17 +86,13 @@
             src_ref=src, dst_ref=dst, send_sem=send, recv_sem=recv, device_id=device, device_id_type=MESH
         )
 
-    def loads(h):
-        cols = pl.ds(h * DH, DH)
-        return [
-            pltpu.make_async_copy(k_hbm.at[:, :, cols], kv_own.at[h, 0], load_sem.at[h, 0]),
-            pltpu.make_async_copy(v_hbm.at[:, :, cols], v_raw.at[h], load_sem.at[h, 1]),
-            pltpu.make_async_copy(q_hbm.at[:, :, cols], q_own.at[h], load_sem.at[h, 2]),
-        ]
-
-    for h in range(HEADS):
-        for copy in loads(h):
-            copy.start()
+    def load(h, part):
+        src = (q_hbm, k_hbm, v_hbm)[part].at[:, :, pl.ds(h * DH, DH)]
+        return pltpu.make_async_copy(src, q_own.at[h] if part == 0 else kv_own.at[h, part - 1], load_sem.at[h, part])
+
+    for part in range(3):
+        for h in range(HEADS):
+            load(h, part).start()
     own_w = pltpu.make_async_copy(
         w_hbm.at[:, pl.ds(pl.multiple_of(x * 512, 512), 512)], wg.at[0], w_sem.at[0, 0]
     )
@@ -123,10 +122,42 @@
         src = kv_own.at[h] if dy == 0 else kv_far.at[h, 2 * dy]
         return remote(src, kv_far.at[h, 2 * dy + 1], ks_sem.at[h, 6 + dy], kr_sem.at[h, 2 * dy + 1], at(0, 0, 1, 0))
 
-    def exc_copy(h, n):
-        dy, dk = mates[n]
-        rel = ((4 - dy) % 4) * 2 + dk - 1
-        return remote(exc_out.at[h], exc_in.at[h, rel], es_sem.at[h, n], er_sem.at[h, rel], at(0, dy, dk, 0))
+    def near(out, into, send, recv, h, dy):
+        slot = 2 * ((4 - dy) % 4) - 1
+        return remote(out.at[h], into.at[h, slot], send.at[h, dy], recv.at[h, slot], at(0, dy, 0, 0))
+
+    def mate(out, into, send, recv, h, dy):
+        src = out.at[h] if dy == 0 else into.at[h, 2 * dy - 1]
+        return remote(src, into.at[h, 2 * dy], send.at[h, 4 + dy], recv.at[h, 2 * dy], at(0, 0, 1, 0))
+
+    def spread_start(arrays, h):
+        mate(*arrays, h, 0).start()
+        for dy in range(1, 4):
+            near(*arrays, h, dy).start()
+
+    def spread_finish(arrays, h):
+        for dy in range(1, 4):
+            near(*arrays, h, 4 - dy).wait_recv()
+            mate(*arrays, h, dy).start()
+        for dy in range(4):
+            mate(*arrays, h, dy).wait_recv()
+
+    def spread_drain(arrays, h):
+        for dy in range(4):
+            mate(*arrays, h, dy).wait_send()
+        for dy in range(1, 4):
+            near(*arrays, h, dy).wait_send()
+
+    exc = (exc_out, exc_in, es_sem, er_sem)
+    handed = (back_out, back_in, bs_sem, br_sem)
+
+    def qx_copy(h, n):
+        return remote(qx_out.at[h, n // 2], qx_in.at[h, n // 2, pl.ds(0, BLK)], qxs_sem.at[h, n // 2],
+                      qxr_sem.at[h, n // 2], at(n + 1, 0, 0, 0))
+
+    def ox_copy(h, n):
+        return remote(qx_in.at[h, n // 2], ox_in.at[h, n // 2], oxs_sem.at[h, n // 2], oxr_sem.at[h, n // 2],
+                      at(PLANES - 1 - n, 0, 0, 0))
 
     def q_copy(h, n):
         return remote(q_out.at[h, n], q_in.at[h, n, pl.ds(0, msg)], qs_sem.at[h, n], qr_sem.at[h, n], at(n + 1, 0, 0, 0))
@@ -134,54 +165,52 @@
     def o_copy(h, n):
         return remote(q_in.at[h, n], o_in.at[h, n], os_sem.at[h, n], or_sem.at[h, n], at(PLANES - 1 - n, 0, 0, 0))
 
-    def back_copy(h, n):
-        dy, dk = mates[n]
-        rel = ((4 - dy) % 4) * 2 + dk - 1
-        return remote(back_out.at[h], back_in.at[h, rel], bs_sem.at[h, n], br_sem.at[h, rel], at(0, dy, dk, 0))
-
     def x_copy(h, d):
         return remote(att.at[0, h], att.at[HEADS - d, h], xs_sem.at[h, d], xr_sem.at[h, HEADS - d], at(0, 0, 0, d))
 
     for h in range(HEADS):
-        for copy in loads(h):
-            copy.wait()
+        load(h, 0).wait()
+    if spare:
+        @pl.loop(0, HEADS)
+        def _(h):
+            for e in range(spare):
+                exc_out[h, e] = q_own[h, table[T_EXC + e]]
+            spread_start(exc, h)
+
+    for h in range(HEADS):
+        for part in (1, 2):
+            load(h, part).wait()
 
     @pl.loop(0, HEADS)
     def _(h):
         @pl.loop(0, BLOCKS)
         def _(b):
-            kv_own[h, 1, b] = v_raw[h, b].T
-
-        if spare:
-            for e in range(spare):
-                exc_out[h, e] = q_own[h, table[T_EXC + e]]
-            for n in range(len(mates)):
-                exc_copy(h, n).start()
+            kv_own[h, 1, b] = kv_own[h, 1, b].T
+            q_all[b] = q_own[h, b]
+
         kv_near(h, 1).start()
         kv_near(h, 3).start()
         kv_mate(h, 0).start()
 
-    for d in range(1, HEADS):
-        w_copy(d).start()
-
-    @pl.loop(0, HEADS)
-    def _(h):
         if spare:
-            for n in range(len(mates)):
-                exc_copy(h, n).wait_recv()
-            for n in range(len(mates)):
+            spread_finish(exc, h)
+            for n in range(NZ):
                 for e in range(spare):
                     q_all[BLOCKS + n * spare + e] = exc_in[h, n, e]
-
-        @pl.loop(0, BLOCKS)
-        def _(b):
-            q_all[b] = q_own[h, b]
 
         @pl.loop(0, NZ)
         def _(n):
             for i in range(cap):
                 q_out[h, n, pl.ds(i * BLK, BLK), :] = q_all[table[T_SEND + n * 8 + i]]
             q_copy(h, n).start()
+            if extra:
+                @pl.when(more(n))
+                def _():
+                    qx_out[h, n // 2] = q_all[table[T_SEND + n * 8 + cap]]
+                    qx_copy(h, n).start()
+
+    for d in range(1, HEADS):
+        w_copy(d).start()
 
     def kv_first(h):
         for part, slot, dy in ((0, 6, 1), (1, 2, 3)):
@@ -225,6 +254,15 @@
                 q_in[h, n, pl.ds(i * BLK, BLK), :] = outs[i]
             q_in[h, n, pl.ds(msg, 16), :] = split_logs(tops, cap)
             o_copy(h, n).start()
+            if extra:
+                @pl.when(more(n))
+                def _():
+                    qx_copy(h, n).wait_recv()
+                    query = qx_in[h, n // 2, pl.ds(0, BLK), :]
+                    out, top = attend(query, *kv_block(table[T_KEY + n * 8 + cap]))
+                    qx_in[h, n // 2, pl.ds(0, BLK), :] = bf(out)
+                    qx_in[h, n // 2, pl.ds(BLK, 16), :] = split_logs([top], 1)
+                    ox_copy(h, n).start()
 
         for j in range(MATES):
             out, top = attend(q_own[h, table[T_IN_Q + j]], *kv_block(table[T_IN_K + j]))
@@ -253,6 +291,12 @@
             for i in range(cap):
                 o_all[n * cap + i] = o_in[h, n, pl.ds(i * BLK, BLK), :]
                 logs[h, n * 8 + i] = both[i : i + 1]
+            if extra:
+                @pl.when(more(n))
+                def _():
+                    ox_copy(h, n).wait_recv()
+                    o_all[base_extra + n // 2] = ox_in[h, n // 2, pl.ds(0, BLK), :]
+                    logs[h, n * 8 + cap] = join_logs(ox_in[h, n // 2, pl.ds(BLK, 16), :])[0:1]
 
         if back:
             tops = []
@@ -260,11 +304,9 @@
                 back_out[h, pl.ds(f * BLK, BLK), :] = o_all[table[T_BACK + f]]
                 tops.append(logs[h, table[T_BACK_LOG + f]])
             back_out[h, pl.ds(back * BLK, 16), :] = split_logs(tops, back)
-            for n in range(len(mates)):
-                back_copy(h, n).start()
-            for n in range(len(mates)):
-                back_copy(h, n).wait_recv()
-            for n in range(len(mates)):
+            spread_start(handed, h)
+            spread_finish(handed, h)
+            for n in range(NZ):
                 both = join_logs(back_in[h, n, pl.ds(back * BLK, 16), :])
                 for f in range(back):
                     o_all[base_back + n * back + f] = back_in[h, n, pl.ds(f * BLK, BLK), :]
@@ -347,25 +389,30 @@
         for n in range(NZ):
             q_copy(h, n).wait_send()
             o_copy(h, n).wait_send()
-        for n in range(len(mates)):
-            if spare:
-                exc_copy(h, n).wait_send()
-            if back:
-                back_copy(h, n).wait_send()
+            if extra:
+                @pl.when(more(n))
+                def _():
+                    qx_copy(h, n).wait_send()
+                    ox_copy(h, n).wait_send()
+        if spare:
+            spread_drain(exc, h)
+        if back:
+            spread_drain(handed, h)
         for d in range(1, HEADS):
             x_copy(h, d).wait_send()
 
 
 def layer(sizes, number, table, queries, keys, values, out_weight):
-    cap, spare, back = sizes
+    cap, extra, spare, back = sizes
     msg = cap * BLK
     tile = (BLK, DH)
+    few = 4 if extra else 1
     b16 = jnp.bfloat16
     dma = pltpu.SemaphoreType.DMA
     any_space = pl.BlockSpec(memory_space=pl.ANY)
     out, _ = pl.pallas_call(
-        functools.partial(layer_kernel, cap, spare, back),
-        name=f"layer_{cap}",
+        functools.partial(layer_kernel, cap, extra, spare, back),
+        name=f"layer_{cap}_{extra}",
         out_shape=(
             jax.ShapeDtypeStruct((ROWS, 512), b16),
             jax.ShapeDtypeStruct((HEADS, MATES, 2, BLOCKS) + tile, b16),
@@ -376,11 +423,13 @@
             pltpu.VMEM((HEADS, BLOCKS) + tile, b16),
             pltpu.VMEM((BLOCKS + NZ * spare,) + tile, b16),
             pltpu.VMEM((HEADS, 2, BLOCKS) + tile, b16),
-            pltpu.VMEM((HEADS, BLOCKS) + tile, b16),
             pltpu.VMEM((HEADS, NZ, msg, DH), b16),
             pltpu.VMEM((HEADS, NZ, msg + 16, DH), b16),
             pltpu.VMEM((HEADS, NZ, msg + 16, DH), b16),
-            pltpu.VMEM((NZ * (cap + back) + MATES,) + tile, b16),
+            pltpu.VMEM((HEADS, few, BLK, DH), b16),
+            pltpu.VMEM((HEADS, few, BLK + 16, DH), b16),
+            pltpu.VMEM((HEADS, few, BLK + 16, DH), b16),
+            pltpu.VMEM((NZ * (cap + back) + 4 * extra + MATES,) + tile, b16),
             pltpu.VMEM((HEADS, max(spare, 1)) + tile, b16),
             pltpu.VMEM((HEADS, NZ, max(spare, 1)) + tile, b16),
             pltpu.VMEM((HEADS, back * BLK + 16, DH), b16),
@@ -395,7 +444,8 @@
             pltpu.VMEM((ROWS, 512), jnp.float32),
             dma((HEADS, 3)), dma((2, HEADS)),
             dma((HEADS, NZ)), dma((HEADS, NZ)), dma((HEADS, NZ)), dma((HEADS, NZ)),
-            dma((HEADS, NZ)), dma((HEADS, NZ)), dma((HEADS, NZ)), dma((HEADS, NZ)),
+            dma((HEADS, 4)), dma((HEADS, 4)), dma((HEADS, 4)), dma((HEADS, 4)),
+            dma((HEADS, 8)), dma((HEADS, NZ)), dma((HEADS, 8)), dma((HEADS, NZ)),
             dma((HEADS, 10)), dma((HEADS, 10)), dma((MATES,)),
             dma((HEADS, HEADS)), dma((HEADS, HEADS)),
         ],
@@ -406,11 +456,60 @@
     return out
 
 
+def swap_kernel(mine, out, every, send_sem, recv_sem):
+    me = lax.axis_index("ctx")
+    x = lax.axis_index("head")
+    z, w = me // MATES, me % MATES
+    planes = [((z + d) % PLANES * MATES + w, x) for d in range(1, PLANES)]
+    mates = [(z * MATES + (w + d) % MATES, x) for d in range(1, MATES)]
+    barrier = pltpu.get_barrier_semaphore()
+    for device in planes + mates:
+        pl.semaphore_signal(barrier, inc=1, device_id=device, device_id_type=MESH)
+    pl.semaphore_wait(barrier, len(planes + mates))
+    every[w, z] = mine[...]
+    for stage, devices, part in ((0, planes, every.at[w, z]), (1, mates, every.at[w])):
+        copies = [
+            pltpu.make_async_remote_copy(
+                src_ref=part, dst_ref=part, send_sem=send_sem.at[stage, n], recv_sem=recv_sem.at[stage, n],
+                device_id=device, device_id_type=MESH,
+            )
+            for n, device in enumerate(devices)
+        ]
+        for copy in copies:
+            copy.start()
+        for copy in copies:
+            copy.wait()
+    out[...] = every[...]
+
+
+def swap(mine):
+    vmem = pl.BlockSpec(memory_space=pltpu.VMEM)
+    shape = (MATES, PLANES, 1, DH)
+    return pl.pallas_call(
+        swap_kernel,
+        name="swap",
+        out_shape=jax.ShapeDtypeStruct(shape, jnp.int32),
+        in_specs=[vmem],
+        out_specs=vmem,
+        scratch_shapes=[
+            pltpu.VMEM(shape, jnp.int32), pltpu.SemaphoreType.DMA((2, 7)), pltpu.SemaphoreType.DMA((2, 7))
+        ],
+        compiler_params=pltpu.CompilerParams(collective_id=3, has_side_effects=True),
+    )(mine)
+
+
 def total(mask, value, axes):
     return jnp.sum(jnp.where(mask, value, 0), axis=axes)
 
 
-def route(places, cap, spare, back):
+def room_of(cap, extra):
+    eight = jnp.arange(8, dtype=jnp.int32)
+    step = (eight - eight[:, None, None]) % 8 - 1
+    more = (step + eight[None, :, None]) % 2 == 0
+    return jnp.where(more, cap + extra, cap)
+
+
+def route(places, cap, extra, spare, back):
     eight = jnp.arange(8, dtype=jnp.int32)
     item = jnp.arange(32, dtype=jnp.int32)
     plane = jnp.where(places >= 0, places // 128, -1)
@@ -420,17 +519,19 @@
     count = jnp.sum(goes, axis=2, dtype=jnp.int32)
     earlier = item[None, :] < item[:, None]
     rank = jnp.sum((plane[..., None, :] == plane[..., :, None]) & earlier, axis=-1, dtype=jnp.int32)
-    over = away & (rank >= cap)
+    limit = room_of(cap, extra)
+    own_limit = total(goes, limit[:, :, None, :], -1)
+    over = away & (rank >= own_limit)
     spare_rank = jnp.sum(over[..., None, :] & earlier, axis=-1, dtype=jnp.int32)
     apart = eight[:, None, None] != eight
-    over_count = jnp.where(apart, jnp.maximum(count - cap, 0), 0)
-    room = jnp.where(apart, jnp.maximum(cap - count, 0), 0)
+    over_count = jnp.where(apart, jnp.maximum(count - limit, 0), 0)
+    room = jnp.where(apart, jnp.maximum(limit - count, 0), 0)
     before = eight[None, :] < eight[:, None]
     over_before = total(before[None, :, :, None], over_count[:, None], 2)
     order = (eight[:, None] - eight[None, :]) % 8
     first = order[None, :, :] < order[:, None, :]
     room_before = total(first[None], room[:, None], 2)
-    turn = total(goes, over_before[:, :, None, :], -1) + rank - cap
+    turn = total(goes, over_before[:, :, None, :], -1) + rank - own_limit
     mine = goes[:, :, :, None, :]
     low = total(mine, room_before[:, None, None], -1)
     size = total(mine, room[:, None, None], -1)
@@ -447,7 +548,7 @@
     return plane, rank, over, spare_rank, carrier, slot, back_rank, jnp.all(fits)
 
 
-def make_table(places, routed, me, cap, spare, back):
+def make_table(places, routed, me, cap, extra, spare, back):
     plane, rank, over, spare_rank, carrier, slot, back_rank, _ = routed
     eight = jnp.arange(8, dtype=jnp.int32)
     item = jnp.arange(32, dtype=jnp.int32)
@@ -488,14 +589,18 @@
     in_q = total(local, item // 2, -1)
     in_k = total(local, key_o, -1)
     rel = relative(carrier_o) - 1
-    place = jnp.where(over_o, 7 * cap + rel * back + back_o, step_o * cap + slot_o)
-    place = jnp.where(inside, 7 * (cap + back) + rank_o, place)
+    def far_place(step, slot):
+        return jnp.where(slot == cap, 7 * cap + step // 2, step * cap + slot)
+
+    base_back = 7 * cap + 4 * extra
+    place = jnp.where(over_o, base_back + rel * back + back_o, far_place(step_o, slot_o))
+    place = jnp.where(inside, base_back + 7 * back + rank_o, place)
     log = jnp.where(over_o, LOG_BACK + rel * 8 + back_o, step_o * 8 + slot_o)
     log = jnp.where(inside, LOG_IN + rank_o, log)
     live = plane_o >= 0
     place, log = jnp.where(live, place, 0), jnp.where(live, log, 0)
     foreign = over_h & (carrier_h == w) & (back_h == eight[:, None, None])
-    back_place = total(foreign, step_h * cap + slot_h, (-1, -2))
+    back_place = total(foreign, far_place(step_h, slot_h), (-1, -2))
     back_log = total(foreign, step_h * 8 + slot_h, (-1, -2))
     pieces = [send.reshape(-1), arrive.reshape(-1), exc, in_q, in_k, place, log, live, back_place, back_log]
     return jnp.concatenate([piece.astype(jnp.int32) for piece in pieces])
@@ -508,17 +613,26 @@
     own_ids = lax.dynamic_slice_in_dim(block_order, me * BLOCKS, BLOCKS)
     where_stored = total(wanted[:, None] == block_order[None, :], stored[None, :], -1)
     mine = jnp.where(wanted != jnp.repeat(own_ids, 2), where_stored, -1)
-    places = lax.all_gather(mine, "ctx").reshape(8, 8, 32)
+    every = swap(jnp.pad(mine, (0, DH - mine.shape[0])).reshape(1, DH))
+    places = jnp.swapaxes(every[:, :, 0, :32], 0, 1)
     arrays = (queries, keys, values, out_weight)
-    routed = route(places, *FAST)
-
-    def fast():
-        return layer(FAST, 0, make_table(places, routed, me, *FAST), *arrays)
-
-    def full():
-        return layer(FULL, 1, make_table(places, route(places, *FULL), me, *FULL), *arrays)
-
-    return lax.cond(routed[-1], fast, full)
+    eight = jnp.arange(8, dtype=jnp.int32)
+    count = jnp.sum((places // 128)[..., None] == eight, axis=2, dtype=jnp.int32)
+    count = jnp.where(eight[:, None, None] != eight, count, 0)
+    many = jnp.sum(count, axis=1) > 8 * SIZES[0][0]
+    over = jnp.sum(jnp.maximum(count - SIZES[0][0], 0), axis=2) > SIZES[0][2]
+    extra = (jnp.any(many) | jnp.any(over)).astype(jnp.int32)
+    routed = route(places, SIZES[0][0], extra, *SIZES[0][2:])
+
+    def variant(number):
+        def run():
+            sizes = SIZES[number]
+            used = route(places, *sizes) if number == 2 else routed
+            return layer(sizes, number, make_table(places, used, me, *sizes), *arrays)
+
+        return run
+
+    return lax.switch(jnp.where(routed[-1], extra, 2), [variant(number) for number in range(3)])
 
 
 def solution(mesh):

time: 413 us -> 351 us (0.85)
  blocking collectives: 44.2 us -> 0 us
  Pallas kernels: 340 us -> 325 us
    all_gather x1 -> x0, blocking collectives: 44.2 us -> none  [shards(): places = lax.all_gather(mine, 'ctx').reshape(8, 8, 32)]
    pallas_call x1 -> x2, Pallas kernels: 340 us -> 325 us  [the longest x1 308 us: layer(): pl.pallas_call(functools.partial(layer_kernel, cap, extra, spare, back),...]
    reduce_sum x11 -> x12, other arithmetic: 8.92 us -> 6.69 us  [total(): return jnp.sum(jnp.where(mask, value, 0), axis=axes)]
where the time goes in v2:
time: 351 us; the launch traced here: 350 us
  Pallas kernels  325 us (93%)
  other arithmetic  15 us (4%)
  local copies, waits for them, and re-layouts  6.74 us (2%)
    pallas_call x1, Pallas kernels, layer(): pl.pallas_call(functools.partial(layer_kernel, cap, extra, spare, back),...  308 us
    pallas_call x1, Pallas kernels, swap(): pl.pallas_call(swap_kernel, name='swap', out_shape=jax.ShapeDtypeStruct(s...  17.5 us

profile of v2, /device:TPU:1, one launch (start us, length us, event | category | flops | bytes accessed | tf_op | source)
XLA Modules:
  0.0 350.2 jit_solution(10352183701048413722)
XLA Ops:
  0.0 0.8 dynamic_slice.192
  0.8 0.1 broadcast_in_dim.595
  0.9 0.1 reshape.1049
  1.0 0.8 copy.86
  1.8 0.1 reshape.1048
  1.8 0.9 select_reduce_fusion.41
  2.7 0.5 pad_bitcast_fusion.mine
  3.3 17.5 %swap.1 = s32[8,8,1,128]{3,2,1,0:T(1,128)S(1)} custom-call(s32[1,128]{1,0:T(1,128)} %pad_bitcast_fusion.mine), custom_call_target="tpu_custom_call" | custom-call | tf_op jit(solution)/shard_map/swap/pallas_call | solution.py:488
  20.9 1.2 convert_reduce_fusion.8
  22.0 0.2 maximum_reduce_fusion
  22.3 0.7 compare_reduce_fusion
  24.4 1.4 convert_reduce_fusion.6
  25.8 1.2 convert_reduce_fusion.7
  27.1 0.2 select_reduce_fusion.38
  27.2 0.2 select_reduce_fusion.37
  27.5 0.1 and.1082
  27.6 0.1 select_reduce_fusion.39
  27.7 1.2 convert_reduce_fusion.5
  28.9 1.5 select_reduce_fusion.34
  30.4 0.2 fusion.182
  30.6 0.1 select_reduce_fusion.36
  30.7 0.1 eq.763
  30.8 0.8 convert_reduce_fusion.4
  31.6 0.1 reshape.1051
  31.7 0.7 fusion.163
  33.0 0.2 broadcast_in_dim.608
  33.3 313.8 %conditional.1 = (bf16[2048,512]{1,0:T(8,128)(2,1)}) conditional(s32[]{:T(128)} %clamp.169, (s32[]{:T(128)}, s32[8,8,32]{2,0,1:T(8,128)S(1)}, s32[8,8,32]{2,0,1:T(8,128)S(1)}, pred[8,8,32,8]{2,3,1,0:T(8,128)(4,1)S(1)}, s32[8,8,8]{2,1,0:T(8,128)S(1)}, /*index=5*/s32[8,8,32,8,8]{2,4,3,1,0:T(8,128)S(1)}, ...), branch_computations={%region_19.29_spmd, %region_29.39_spmd, %region_39.60_spmd} | conditional | flops 4899041 | bytes 1119420 | solution.py:635
  33.6 0.1 compare_and_fusion
  33.8 0.1 broadcast_and_fusion
  34.0 0.9 select_reduce_fusion
  34.9 0.2 select_reduce_fusion.2
  35.0 0.1 fusion.9
  35.2 0.2 select_reduce_fusion.6
  35.4 0.4 select_reduce_fusion.4
  35.8 1.1 select_reduce_fusion.3
  36.9 0.1 reshape.1028
  37.1 1.1 select_reduce_fusion.1
  38.2 0.1 reshape.1029
  38.2 0.7 concatenate.6.table
  38.9 307.9 %layer_5_0.2 = (bf16[2048,512]{1,0:T(8,128)(2,1)}, bf16[4,8,2,16,128,128]{5,4,3,2,1,0:T(8,128)(2,1)}) custom-call(s32[248]{0:T(256)} %concatenate.6.table, bf16[16,128,512]{2,1,0:T(8,128)(2,1)} %bitcast.16.q_hbm, bf16[16,128,512]{2,1,0:T(8,128)(2,1)} %bitcast.17.k_hbm, bf16[16,128,512]{2,1,0:T(8,128)(2,1)} %bitcast.18.v_hbm, ...), custom_call_target="tpu_custom_call" | custom-call | tf_op jit(solution)/shard_map/cond/branch_0_fun/layer_5_0/pallas_call | solution.py:413
  347.1 3.0 copy.155
  (41 shorter events, 0.6 us)
